TPU v7x, 256 devices: a whole 4x4x8 slice. The times are simulated.
256 devices in a mesh: gr: 32 (over z_lo, x, y), gc: 8 (over z_hi, core).
Axes of the slice: x: 4, y: 4, z: 8 (z_hi: 4, z_lo: 2; z = z_hi * 2 + z_lo), core: 2. Of those that a mesh axis runs over, the one named last changes fastest.
Arguments:
- alignment_matrix: bfloat16 [512, 1536, 64], P(('gr', 'gc')), may hold values from -24 to 24
- sequence_validity: int32 [512], replicated, may hold values from 0 to 1, as said below
- residue_validity: int32 [1536], replicated, may hold values 0 or 1
- standardize_gain: float32 [64], replicated, may hold values from 0.1 to 1.9
- standardize_offset: float32 [64], replicated, may hold values from -3 to 3
- first_projector: bfloat16 [64, 32], replicated, may hold values from -0.75 to 0.75
- second_projector: bfloat16 [64, 32], replicated, may hold values from -0.75 to 0.75
- final_projector: bfloat16 [1024, 128], replicated, may hold values from -2 to 2
- final_offset: float32 [128], replicated, may hold values from -3 to 3
Outputs:
- pair_update: bfloat16 [1536, 1536, 128], P('gr', 'gc')
Inputs may be any that keep to these rules, and one draw needn't show every extreme that they name: `sequence_validity`: each entry is 0 or 1; the first row is always 1.
All inputs are finite; a program needn't handle non-finite values.
Results may differ from a plain program's by a relative error of at most 0.0052.
Values may be sent and summed in bfloat16 or wider, within the bound.
A program may use at most 128 MiB of HBM per device.

v0:
```python
import jax
import jax.numpy as jnp
from jax import lax
from jax.sharding import PartitionSpec as P


def standardize_features(input_entries, gain, shift):
    input_entries = input_entries.astype(jnp.float32)
    center = jnp.mean(input_entries, axis=-1, keepdims=True)
    spread = jnp.mean((input_entries - center) ** 2, axis=-1, keepdims=True)
    return (input_entries - center) * lax.rsqrt(spread + 1e-05) * gain + shift


def on_device(
    alignment_matrix,
    sequence_validity,
    residue_validity,
    standardize_gain,
    standardize_offset,
    first_projector,
    second_projector,
    final_projector,
    final_offset,
):
    sequence_number, residue_number, feature_number = alignment_matrix.shape
    hidden = first_projector.shape[1]
    width_z = final_projector.shape[1]
    n_rows = lax.axis_size("gr")
    n_cols = lax.axis_size("gc")
    per_device = residue_number // (n_rows * n_cols)
    row_tok = per_device * n_cols
    col_tok = per_device * n_rows
    standardized_alignment = standardize_features(
        alignment_matrix, standardize_gain, standardize_offset
    ).astype(jnp.bfloat16)
    weights = jnp.concatenate([first_projector, second_projector], axis=1)
    both = jnp.dot(
        standardized_alignment.reshape(sequence_number * residue_number, feature_number),
        weights,
        preferred_element_type=jnp.float32,
    )
    both = (
        both.reshape(sequence_number, residue_number, 2 * hidden)
        * residue_validity.astype(jnp.float32)[None, :, None]
    )
    both = both.astype(jnp.bfloat16)
    left_send = both[:, :, :hidden].reshape(sequence_number, n_rows, n_cols, per_device * hidden)
    right_send = (
        both[:, :, hidden:]
        .reshape(sequence_number, n_cols, n_rows, per_device * hidden)
        .transpose(0, 2, 1, 3)
    )
    packed = jnp.concatenate([left_send, right_send], axis=3)
    moved = lax.all_to_all(
        lax.all_to_all(packed, "gr", split_axis=1, concat_axis=1, tiled=True),
        "gc",
        split_axis=2,
        concat_axis=2,
        tiled=True,
    )
    moved = moved.transpose(1, 2, 0, 3).reshape(-1, 2 * per_device * hidden)
    sequence_share = lax.all_gather(moved[:, : per_device * hidden], "gc", axis=1, tiled=True)
    col_part = lax.all_gather(moved[:, per_device * hidden :], "gr", axis=1, tiled=True)
    sequence_share = sequence_share * sequence_validity.astype(jnp.bfloat16)[:, None]
    divisor_sum = jnp.sum(sequence_validity.astype(jnp.float32))
    weight3 = final_projector.reshape(hidden, hidden, width_z)
    block = 16
    nblocks = row_tok // block

    def one_block(index):
        piece = lax.dynamic_slice_in_dim(sequence_share, index * block * hidden, block * hidden, 1)
        outer = lax.dot_general(
            piece, col_part, (((0,), (0,)), ((), ())), preferred_element_type=jnp.float32
        )
        outer = outer.astype(jnp.bfloat16).reshape(block, hidden, col_tok, hidden)
        projected = jnp.einsum("icjd,cdz->ijz", outer, weight3, preferred_element_type=jnp.float32)
        return (projected / divisor_sum + final_offset).astype(jnp.bfloat16)

    result = lax.map(one_block, jnp.arange(nblocks, dtype=jnp.int32))
    return result.reshape(row_tok, col_tok, width_z)


def solution(mesh):
    in_specs = (P(("gr", "gc"), None, None), P(), P(), P(), P(), P(), P(), P(), P())
    out_specs = P("gr", "gc", None)
    return jax.shard_map(
        on_device, mesh=mesh, in_specs=in_specs, out_specs=out_specs, check_vma=False
    )
```

profile of v0, /device:TPU:2, one launch (start us, length us, event | category | flops | bytes accessed | tf_op | source)
XLA Modules:
  0.0 404.6 jit_solution(11000664290131862238)
XLA Ops:
  6.5 1.1 convert_reduce_fusion
  7.6 1.1 fusion.10
  8.8 0.7 convert_element_type.32
  9.5 1.4 fusion.7
  10.9 0.4 copy.22
  11.3 0.6 reshape.45
  12.0 0.4 copy.21
  12.4 0.6 reshape.44
  13.2 17.8 %all_to_all.10 = bf16[2,32,8,384]{3,2,0,1:T(8,128)(2,1)S(1)} all-to-all(bf16[2,32,8,384]{3,2,0,1:T(8,128)(2,1)S(1)} %copy.24), channel_id=1, replica_groups=mesh['gr'=32,'gc'=8] {'gr'}, dimensions={1} | all-to-all | bytes 786432 | tf_op jit(solution)/shard_map/all_to_all | solution.py:55
  31.1 22.6 %all_to_all.11 = bf16[2,32,8,384]{3,1,0,2:T(8,128)(2,1)S(1)} all-to-all(bf16[2,32,8,384]{3,1,0,2:T(8,128)(2,1)S(1)} %copy.25), channel_id=1, replica_groups=mesh['gr'=32,'gc'=8] {'gc'}, dimensions={2} | all-to-all | bytes 786432 | tf_op jit(solution)/shard_map/all_to_all | solution.py:54
  53.7 0.3 copy.26
  54.3 0.8 copy.27
  55.2 0.2 all-gather.5.cloned.1.call-start
  55.4 0.8 copy.28
  56.3 0.6 convert_reduce_fusion.1
  56.9 25.0 %all-gather.3.cloned.1.call-done = bf16[512,1536]{0,1:T(8,128)(2,1)} async-done(((bf16[512,192]{0,1:T(8,128)(2,1)}), bf16[512,1536]{0,1:T(8,128)(2,1)}) %all-gather.3.cloned.1.call-update) | async-done | bytes 1572880 | tf_op jit(solution)/shard_map/all_gather | solution.py:62
  81.9 1.5 broadcast_multiply_fusion
  83.4 159.5 %all-gather.5.cloned.1.call-done = bf16[512,6144]{0,1:T(8,128)(2,1)} async-done(((bf16[512,192]{0,1:T(8,128)(2,1)}), bf16[512,6144]{0,1:T(8,128)(2,1)}) %all-gather.5.cloned.1.call-update) | async-done | bytes 6291472 | tf_op jit(solution)/shard_map/all_gather | solution.py:63
  242.9 8.7 %copy.30 = bf16[512,6144]{1,0:T(8,128)(2,1)} copy(bf16[512,6144]{0,1:T(8,128)(2,1)} %all-gather.5.cloned.1.call-done) | data formatting | bytes 12582912 | tf_op jit(solution)/shard_map/while | solution.py:79
  251.6 146.1 %while.12 = (s32[]{:T(128)}, bf16[3,16,192,128]{3,2,1,0:T(8,128)(2,1)}, s32[3]{0:T(128)S(1)}, bf16[512,1536]{0,1:T(8,128)(2,1)S(1)}, bf16[512,6144]{1,0:T(8,128)...) while((s32[]{:T(128)}, ...), condition=%wide.region_4.5_spmd, body=%wide.region_3.4_spmd.sunk | while | flops 4030857216 | bytes 51906224 | solution.py:79
  251.6 0.6 dynamic_slice.18
  252.9 8.2 %convolution_convert_fusion.2 = bf16[512,6144]{1,0:T(8,128)(2,1)} fusion(bf16[512,6144]{1,0:T(8,128)(2,1)} %get-tuple-element.212, bf16[512,1536]{0,1:T(8,128)(2,1)S(1)} %get-tuple-element.211, s32[]{:T(128)S(6)} %select_n.7), kind=kOutput, calls=%fused_computation.clone.1 | convolution fusion | flops 3224371200 | bytes 13107204 | tf_op jit(solution)/shard_map/while/body/eval_jaxpr/dot_general | solution.py:72
  261.1 24.6 %reshape.53 = bf16[16,32,192,32]{3,2,1,0:T(8,128)(2,1)} reshape(bf16[512,6144]{1,0:T(8,128)(2,1)} %convolution_convert_fusion.2) | data formatting | bytes 12582912 | tf_op jit(solution)/shard_map/while/body/eval_jaxpr/reshape | solution.py:75
  285.6 14.7 %fusion.35 = bf16[3,16,192,128]{3,2,1,0:T(8,128)(2,1)} fusion(bf16[3,16,192,128]{3,2,1,0:T(8,128)(2,1)} %get-tuple-element.197, s32[]{:T(128)} %get-tuple-element.196, bf16[16,32,192,32]{3,2,1,0:T(8,128)(2,1)} %reshape.53, f32[128]{0:T(128)S(1)} %get-tuple-element.215, f32[]{:T(128)} %get-tuple-element.214, ...), kind=kOutput, calls=%fused_computation.5.clone.1 | convolution fusion | flops 806486016 | bytes 26215936 | tf_op jit(solution)/shard_map/while/body/eval_jaxpr/icjd,cdz->ijz/dot_general | solution.py:76
  300.3 0.6 dynamic_slice.18
  301.6 8.2 %convolution_convert_fusion.2 = bf16[512,6144]{1,0:T(8,128)(2,1)} fusion(bf16[512,6144]{1,0:T(8,128)(2,1)} %get-tuple-element.212, bf16[512,1536]{0,1:T(8,128)(2,1)S(1)} %get-tuple-element.211, s32[]{:T(128)S(6)} %select_n.7), kind=kOutput, calls=%fused_computation.clone.1 | convolution fusion | flops 3224371200 | bytes 13107204 | tf_op jit(solution)/shard_map/while/body/eval_jaxpr/dot_general | solution.py:72
  309.8 24.6 %reshape.53 = bf16[16,32,192,32]{3,2,1,0:T(8,128)(2,1)} reshape(bf16[512,6144]{1,0:T(8,128)(2,1)} %convolution_convert_fusion.2) | data formatting | bytes 12582912 | tf_op jit(solution)/shard_map/while/body/eval_jaxpr/reshape | solution.py:75
  334.3 14.7 %fusion.35 = bf16[3,16,192,128]{3,2,1,0:T(8,128)(2,1)} fusion(bf16[3,16,192,128]{3,2,1,0:T(8,128)(2,1)} %get-tuple-element.197, s32[]{:T(128)} %get-tuple-element.196, bf16[16,32,192,32]{3,2,1,0:T(8,128)(2,1)} %reshape.53, f32[128]{0:T(128)S(1)} %get-tuple-element.215, f32[]{:T(128)} %get-tuple-element.214, ...), kind=kOutput, calls=%fused_computation.5.clone.1 | convolution fusion | flops 806486016 | bytes 26215936 | tf_op jit(solution)/shard_map/while/body/eval_jaxpr/icjd,cdz->ijz/dot_general | solution.py:76
  349.0 0.6 dynamic_slice.18
  350.3 8.2 %convolution_convert_fusion.2 = bf16[512,6144]{1,0:T(8,128)(2,1)} fusion(bf16[512,6144]{1,0:T(8,128)(2,1)} %get-tuple-element.212, bf16[512,1536]{0,1:T(8,128)(2,1)S(1)} %get-tuple-element.211, s32[]{:T(128)S(6)} %select_n.7), kind=kOutput, calls=%fused_computation.clone.1 | convolution fusion | flops 3224371200 | bytes 13107204 | tf_op jit(solution)/shard_map/while/body/eval_jaxpr/dot_general | solution.py:72
  358.5 24.6 %reshape.53 = bf16[16,32,192,32]{3,2,1,0:T(8,128)(2,1)} reshape(bf16[512,6144]{1,0:T(8,128)(2,1)} %convolution_convert_fusion.2) | data formatting | bytes 12582912 | tf_op jit(solution)/shard_map/while/body/eval_jaxpr/reshape | solution.py:75
  383.0 14.7 %fusion.35 = bf16[3,16,192,128]{3,2,1,0:T(8,128)(2,1)} fusion(bf16[3,16,192,128]{3,2,1,0:T(8,128)(2,1)} %get-tuple-element.197, s32[]{:T(128)} %get-tuple-element.196, bf16[16,32,192,32]{3,2,1,0:T(8,128)(2,1)} %reshape.53, f32[128]{0:T(128)S(1)} %get-tuple-element.215, f32[]{:T(128)} %get-tuple-element.214, ...), kind=kOutput, calls=%fused_computation.5.clone.1 | convolution fusion | flops 806486016 | bytes 26215936 | tf_op jit(solution)/shard_map/while/body/eval_jaxpr/icjd,cdz->ijz/dot_general | solution.py:76
  (21 shorter events, 0.8 us)
Async XLA Ops:
  6.5 75.4 %all-gather.3.cloned.1.call-start = ((), (), s32[]{:S(2)}) async-start(), calls=%async_computation.2 | async-start | bytes 1769472 | tf_op jit(solution)/shard_map/all_gather | solution.py:62
  31.1 25.1 %copy-start = (s32[512]{0:T(512)S(1)}, s32[512]{0:T(512)}, u32[]{:S(2)}) copy-start(s32[512]{0:T(512)} %param.12) | copy-start | bytes 6148
  55.2 187.8 %all-gather.5.cloned.1.call-start = ((), (), s32[]{:S(2)}) async-start(), calls=%async_computation.3 | async-start | bytes 6488064 | tf_op jit(solution)/shard_map/all_gather | solution.py:63
  83.4 168.2 %copy-start.1 = (bf16[1024,128]{1,0:T(8,128)(2,1)S(1)}, bf16[1024,128]{1,0:T(8,128)(2,1)}, u32[]{:S(2)}) copy-start(bf16[1024,128]{1,0:T(8,128)(2,1)} %param.18) | copy-start | bytes 786436
  83.4 168.2 %copy-start.2 = (f32[128]{0:T(128)S(1)}, f32[128]{0:T(128)}, u32[]{:S(2)}) copy-start(f32[128]{0:T(128)} %param.19) | copy-start | bytes 1540
Sparse Core Ops, SparseCore 0:
  55.3 26.5 all-gather.2
  83.7 159.2 all-gather.4
where the time goes:
time: 412 us; the launch traced here: 405 us
  waiting for transfers between devices  185 us (45%)
  local copies, waits for them, and re-layouts  88.7 us (22%)
  matrix products  70 us (17%)
  blocking collectives  40.5 us (10%)
  between operations  13.6 us (3%)
  other arithmetic  5.24 us (1%)
    all_gather x1, waiting for transfers between devices, on_device(): lax.all_gather(moved[:, per_device * hidden:], 'gr', axis=1, tiled=True)  160 us
    reshape x3, local copies, waits for them, and re-layouts, one_block(): outer = outer.astype(jnp.bfloat16).reshape(block, hidden, col_tok, hidden)  73.7 us
    dot_general x3, matrix products, one_block(): jnp.einsum('icjd,cdz->ijz', outer, weight3, preferred_element_type=jnp.fl...  44.1 us
    all_gather x1, waiting for transfers between devices, on_device(): lax.all_gather(moved[:, :per_device * hidden], 'gc', axis=1, tiled=True)  25 us
    dot_general x3, matrix products, one_block(): lax.dot_general(piece, col_part, (((0,), (0,)), ((), ())), preferred_elem...  24.5 us
    all_to_all x1, blocking collectives, on_device(): lax.all_to_all(lax.all_to_all(packed, 'gr', split_axis=1, concat_axis=1,...  22.6 us
    all_to_all x1, blocking collectives, on_device(): lax.all_to_all(packed, 'gr', split_axis=1, concat_axis=1, tiled=True)  17.8 us
    while x1, local copies, waits for them, and re-layouts, on_device(): result = lax.map(one_block, jnp.arange(nblocks, dtype=jnp.int32))  8.67 us
  transfers between devices with their start and end apart: 2, of which 2 were waited for; matrix products, arithmetic and copies ran while one was open for 1% of the time, Pallas kernels for 0%

commit v1 on v0

v1 whole, which is shorter than its diff:
```python
import functools
import jax
import jax.numpy as jnp
from jax import lax
from jax.experimental import pallas as pl
from jax.experimental.pallas import tpu as pltpu
from jax.sharding import PartitionSpec as P

F32 = jnp.float32
BF16 = jnp.bfloat16
MESH = pl.DeviceIdType.MESH
NT = (((1,), (1,)), ((), ()))


def iota(shape, dim):
    return lax.broadcasted_iota(jnp.int32, shape, dim)


def ones_where(cond):
    return jnp.where(cond, 1.0, 0.0).astype(BF16)


def dot(a, b):
    return jnp.dot(a, b, preferred_element_type=F32)


def dot_nt(a, b):
    return lax.dot_general(a, b, NT, preferred_element_type=F32)


def where_am_i():
    gr = lax.axis_index("gr")
    gc = lax.axis_index("gc")
    zl = gr // 16
    pos = gr % 16
    zc = ((gc // 2) * 2 + zl) * 2 + gc % 2
    return gr, gc, zl, pos, zc


def ring_device(zl_to_gr, zc):
    z = zc // 2
    return {"gr": (z % 2) * 16 + zl_to_gr, "gc": (z // 2) * 2 + zc % 2}


def plane_device(zl, gc, pos):
    return {"gr": zl * 16 + pos, "gc": gc}


def comm_kernel(
    sv_smem, msa_ref, rv_ref, gain_ref, off_ref, w1_ref, w2_ref,
    rg, lg,
    rs, rb, ls, la, lb, nf, lq, lsf, gainv,
    rs_send, rs_recv, ls_send, ls_recv, lz_send, lz_recv, lt_send, lt_recv,
    g_send, g_recv,
):
    gr, gc, zl, pos, zc = where_am_i()
    core = gc % 2
    px, py = pos // 4, pos % 4

    barrier = pltpu.get_barrier_semaphore()

    @pl.loop(1, 16)
    def _(o):
        pl.semaphore_signal(barrier, inc=1, device_id=ring_device(pos, (zc + o) % 16), device_id_type=MESH)
        pl.semaphore_signal(barrier, inc=1, device_id=plane_device(zl, gc, (pos + o) % 16), device_id_type=MESH)

    k = iota((64, 128), 0)
    lane = iota((64, 128), 1)
    both = [
        jnp.where(lane // 64 == r, jnp.where(lane % 64 == k, 1.0, 0.0) - 1.0 / 64, 0.0).astype(BF16)
        for r in range(2)
    ]
    mean2 = jnp.where(iota((128, 128), 0) // 64 == iota((128, 128), 1) // 64, 1.0 / 64, 0.0).astype(BF16)
    t1 = ones_where(iota((512, 64), 0) % 64 == iota((512, 64), 1))
    t2 = ones_where(iota((32, 256), 1) % 32 == iota((32, 256), 0))
    row, col = iota((512, 256), 0), iota((512, 256), 1)
    wl = dot(dot(t1, w1_ref[...]).astype(BF16), t2)
    wl = jnp.where((row // 128 == (col // 32) % 4) & ((row // 64) % 2 == col // 128), wl, 0.0).astype(BF16)
    t3 = ones_where(iota((64, 32), 0) % 32 == iota((64, 32), 1))
    t4 = ones_where(iota((64, 128), 1) % 64 == iota((64, 128), 0))
    wr = dot(dot_nt(t3, w2_ref[...]).astype(BF16), t4)
    wr = jnp.where(iota((64, 128), 0) // 32 == iota((64, 128), 1) // 64, wr, 0.0).astype(BF16)
    gainv[0:1, 0:64] = gain_ref[...]
    gainv[0:1, 64:128] = gain_ref[...]
    gainv[1:2, 0:64] = off_ref[...]
    gainv[1:2, 64:128] = off_ref[...]
    sv0 = sv_smem[(gr * 8 + gc) * 2].astype(F32)
    sv1 = sv_smem[(gr * 8 + gc) * 2 + 1].astype(F32)
    svm = jnp.where(iota((64, 384), 0) < 32, sv0, sv1)
    low = iota((16, 128), 1) < 64

    @pl.loop(0, 4)
    def _(g):
        rows = pl.ds(pl.multiple_of(g * 384, 384), 384)
        d = dot(msa_ref[0, rows, :], both[0]) + dot(msa_ref[1, rows, :], both[1])
        dd = d * d
        hi = dd.astype(BF16)
        lo = (dd - hi.astype(F32)).astype(BF16)
        var = dot(hi, mean2) + dot(lo, mean2)
        n = (d * lax.rsqrt(var + 1e-05) * gainv[0:1, :] + gainv[1:2, :]).astype(BF16)
        nf[rows, :] = n.astype(F32)
        y = dot_nt(wr, n) * svm * rv_ref[g].astype(F32)
        for r in range(2):
            yr = y[r * 32 : r * 32 + 32]
            a, b = yr[0:16, 128:256], yr[16:32, 128:256]
            rs[2 * g, 0, r] = yr[0:16, 0:128].astype(BF16)
            rs[2 * g, 1, r] = yr[16:32, 0:128].astype(BF16)
            rs[2 * g, 2, r] = jnp.where(low, a, pltpu.roll(b, 64, axis=1)).astype(BF16)
            rs[2 * g + 1, 0, r] = yr[0:16, 256:384].astype(BF16)
            rs[2 * g + 1, 1, r] = yr[16:32, 256:384].astype(BF16)
            rs[2 * g + 1, 2, r] = jnp.where(low, pltpu.roll(a, 64, axis=1), b).astype(BF16)

    x4 = jnp.concatenate([nf[pl.ds(m, 384, stride=4), :] for m in range(4)], axis=1).astype(BF16)
    left = dot(x4, wl)
    lq[0] = left[:, 0:128]
    lq[1] = left[:, 128:256]
    for p in range(16):
        for l in range(2):
            for r in range(2):
                at = 12 * (l * 16 + p)
                lsf[p, l * 24 + r * 12 : l * 24 + r * 12 + 12, :] = lq[r, at : at + 12, :]
    ls[...] = lsf[...].astype(BF16)

    pl.semaphore_wait(barrier, 30)

    def rs_copy(p, o):
        to = (zc + o) % 16
        dev = ring_device(pos, to)
        return pltpu.make_async_remote_copy(
            src_ref=rs.at[dev["gc"], p], dst_ref=rb.at[p, zc],
            send_sem=rs_send.at[p, o], recv_sem=rs_recv.at[p, o],
            device_id=dev, device_id_type=MESH)

    def rs_wait(p, o):
        frm = (zc - o + 16) % 16
        return pltpu.make_async_remote_copy(
            src_ref=rs.at[0, p], dst_ref=rb.at[p, frm],
            send_sem=rs_send.at[p, o], recv_sem=rs_recv.at[p, o],
            device_id=ring_device(pos, frm), device_id_type=MESH)

    def ls_copy(o):
        to = (pos + o) % 16
        return pltpu.make_async_remote_copy(
            src_ref=ls.at[to], dst_ref=la.at[pos],
            send_sem=ls_send.at[o], recv_sem=ls_recv.at[o],
            device_id=plane_device(zl, gc, to), device_id_type=MESH)

    def ls_wait(o):
        frm = (pos - o + 16) % 16
        return pltpu.make_async_remote_copy(
            src_ref=ls.at[0], dst_ref=la.at[frm],
            send_sem=ls_send.at[o], recv_sem=ls_recv.at[o],
            device_id=plane_device(zl, gc, frm), device_id_type=MESH)

    @pl.loop(1, 16)
    def _(o):
        rs_copy(0, o).start()

    @pl.loop(1, 16)
    def _(o):
        ls_copy(o).start()

    for p in range(1, 3):

        @pl.loop(1, 16)
        def _(o, p=p):
            rs_copy(p, o).start()

    for p in range(3):
        rb[p, zc] = rs[gc, p]
    la[pos] = ls[pos]

    def flat(x, y):
        return ((x + 4) % 4) * 4 + (y + 4) % 4

    def along(half, a, b):
        return flat(px + a, py + b) if half == 0 else flat(px + b, py + a)

    def g_copy(p, half, sem, who, part, da, db):
        t0, tn = {"all": (0, 8), "lo": (0, 4), "hi": (4, 4)}[part]
        t = pl.ds(16 * p + 8 * half + t0, tn)
        return pltpu.make_async_remote_copy(
            src_ref=rg.at[who, t], dst_ref=rg.at[who, t],
            send_sem=g_send.at[p, half, sem], recv_sem=g_recv.at[p, half, sem],
            device_id=plane_device(zl, gc, along(half, da, db)), device_id_type=MESH)

    sent = []

    def send(*args):
        c = g_copy(*args)
        c.start()
        sent.append(c)

    def stage1_start(p, half):
        me = along(half, 0, 0)
        send(p, half, 0, me, "all", 1, 0)
        send(p, half, 1, me, "all", -1, 0)

    def stage1_forward(p, half):
        g_copy(p, half, 0, along(half, -1, 0), "all", 1, 0).wait_recv()
        send(p, half, 2, along(half, -1, 0), "lo", 1, 0)
        g_copy(p, half, 1, along(half, 1, 0), "all", -1, 0).wait_recv()
        send(p, half, 3, along(half, 1, 0), "hi", -1, 0)

    def stage1_end(p, half):
        g_copy(p, half, 2, along(half, 2, 0), "lo", 1, 0).wait_recv()
        g_copy(p, half, 3, along(half, 2, 0), "hi", -1, 0).wait_recv()

    shifts = (0, -1, 1, 2)

    def stage2_start(p, half, u):
        s = 4 + 4 * u
        who = along(half, shifts[u], 0)
        send(p, half, s, who, "all", 0, 1)
        send(p, half, s + 1, who, "all", 0, -1)

    def stage2_forward(p, half, u):
        s = 4 + 4 * u
        minus, plus = along(half, shifts[u], -1), along(half, shifts[u], 1)
        g_copy(p, half, s, minus, "all", 0, 1).wait_recv()
        send(p, half, s + 2, minus, "lo", 0, 1)
        g_copy(p, half, s + 1, plus, "all", 0, -1).wait_recv()
        send(p, half, s + 3, plus, "hi", 0, -1)

    def stage2_end(p, half, u):
        s = 4 + 4 * u
        g_copy(p, half, s + 2, along(half, shifts[u], 2), "lo", 0, 1).wait_recv()
        g_copy(p, half, s + 3, along(half, shifts[u], 2), "hi", 0, -1).wait_recv()

    o0, i0 = iota((512, 1), 0), iota((512, 512), 1)
    perm0 = ones_where((o0 % 32) * 16 + o0 // 32 == i0)

    def assemble_right(p):
        @pl.loop(1, 16)
        def _(o):
            rs_wait(p, o).wait_recv()

        x = rb[p].reshape(512, 128)
        rg[pos, 16 * p : 16 * p + 16] = dot(perm0, x).astype(BF16).reshape(16, 32, 128)

    def assemble_left():
        @pl.loop(1, 16)
        def _(o):
            ls_wait(o).wait_recv()

        o1, i1 = iota((768, 1), 0), iota((768, 768), 1)
        lq1 = o1 // 32
        l1 = jnp.where(lq1 >= 12, 1, 0)
        at = ((o1 // 2) % 16) * 48 + l1 * 24 + (o1 % 2) * 12 + (lq1 - 12 * l1)
        perm1 = ones_where(at == i1)
        y = dot(perm1, la[...].reshape(768, 128)).astype(BF16)
        lb[...] = y.reshape(2, 12, 32, 128)
        lg[zc] = lb[zl]

    def lz_copy(o):
        to = (zc + 2 * o) % 16
        return pltpu.make_async_remote_copy(
            src_ref=lb.at[(to // 2) % 2], dst_ref=lg.at[zc],
            send_sem=lz_send.at[o], recv_sem=lz_recv.at[o],
            device_id=ring_device(pos, to), device_id_type=MESH)

    def lz_wait(o):
        frm = (zc - 2 * o + 16) % 16
        return pltpu.make_async_remote_copy(
            src_ref=lb.at[0], dst_ref=lg.at[frm],
            send_sem=lz_send.at[o], recv_sem=lz_recv.at[o],
            device_id=ring_device(pos, frm), device_id_type=MESH)

    twin = {"gr": gr, "gc": gc + 1 - 2 * core}

    def lt_copy(o):
        frm = (zc - 2 * o + 16) % 16
        return pltpu.make_async_remote_copy(
            src_ref=lg.at[frm], dst_ref=lg.at[frm],
            send_sem=lt_send.at[o], recv_sem=lt_recv.at[o],
            device_id=twin, device_id_type=MESH)

    def lt_wait(o):
        frm = (zc + 1 - 2 * core - 2 * o + 16) % 16
        return pltpu.make_async_remote_copy(
            src_ref=lg.at[frm], dst_ref=lg.at[frm],
            send_sem=lt_send.at[o], recv_sem=lt_recv.at[o],
            device_id=twin, device_id_type=MESH)

    assemble_right(0)
    for h in range(2):
        stage1_start(0, h)
    assemble_left()

    @pl.loop(1, 8)
    def _(o):
        lz_copy(o).start()

    lt_copy(0).start()
    for h in range(2):
        stage1_forward(0, h)
        stage2_start(0, h, 0)
    for h in range(2):
        for u in (1, 2):
            stage2_start(0, h, u)
    assemble_right(1)
    for h in range(2):
        stage1_start(1, h)
    assemble_right(2)
    for h in range(2):
        stage1_end(0, h)
        stage2_start(0, h, 3)
    for p in range(3):
        for h in range(2):
            stage2_forward(p, h, 0)
        if p < 2:
            for h in range(2):
                stage1_forward(p + 1, h)
                for u in range(3):
                    stage2_start(p + 1, h, u)
            if p < 1:
                for h in range(2):
                    stage1_start(2, h)
        for u in (1, 2, 3):
            for h in range(2):
                stage2_forward(p, h, u)
        if p < 2:
            for h in range(2):
                stage1_end(p + 1, h)
                stage2_start(p + 1, h, 3)
        for u in range(4):
            for h in range(2):
                stage2_end(p, h, u)
        if p == 0:

            @pl.loop(1, 8)
            def _(o):
                lz_wait(o).wait_recv()
                lt_copy(o).start()

    @pl.loop(0, 8)
    def _(o):
        lt_wait(o).wait_recv()

    for c in sent:
        c.wait_send()

    @pl.loop(1, 16)
    def _(o):
        ls_copy(o).wait_send()
        for p in range(3):
            rs_copy(p, o).wait_send()

    @pl.loop(1, 8)
    def _(o):
        lz_copy(o).wait_send()

    @pl.loop(0, 8)
    def _(o):
        lt_copy(o).wait_send()


def tile_kernel(
    rv_smem, sv_ref, rg, lg, fp_ref, off_ref,
    out_ref,
    fpf, wd, wt, lt, outer, acc,
):
    gr = lax.axis_index("gr")
    core = lax.axis_index("gc") % 2
    eye = ones_where(iota((128, 128), 0) == iota((128, 128), 1))
    fpf[...] = fp_ref[...].astype(F32)
    for d in range(32):
        wd[32 * d : 32 * d + 32, :] = fpf[pl.ds(d, 32, stride=32), :].astype(BF16)
    wfull = dot_nt(eye, wd[...]).astype(BF16)
    wt[0:128, :] = wfull[:, 0:512]
    wt[128:256, :] = wfull[:, 512:1024]
    o2, i2 = iota((512, 1), 0), iota((512, 512), 1)
    perm2 = ones_where(((o2 // 2) % 16) * 32 + (o2 // 32) * 2 + o2 % 2 == i2)

    @pl.loop(0, 12)
    def _(q):
        y = dot(perm2, lg[:, q].reshape(512, 128)).astype(BF16)
        lt[pl.ds(pl.multiple_of(q * 128, 128), 128), :] = dot_nt(eye, y).astype(BF16)

    count = jnp.sum(sv_ref[...].astype(F32))
    inv = 1.0 / jnp.full((1, 128), count, F32)
    off_a = pl.multiple_of(64 * core, 64)
    off_b = pl.multiple_of(128 - 128 * core, 64)

    for p in range(3):

        @pl.loop(0, 6)
        def _(ib, p=p):
            x = lt[pl.ds(pl.multiple_of(ib * 256, 256), 256), :]
            for t in range(0, 16, 2):
                w = jnp.concatenate(
                    [rg[:, 16 * p + t + e].reshape(512, 128) for e in range(2)], axis=1)
                s = dot(x, w).astype(BF16)
                for i in range(8):
                    for e in range(2):
                        outer[i, t + e] = s[i * 32 : i * 32 + 32, e * 128 : e * 128 + 128]
            for i in range(0, 8, 2):
                w = jnp.concatenate([outer[i + e].reshape(512, 128) for e in range(2)], axis=1)
                if p == 0:
                    y = dot(wt[0:128, :], w)
                    for e in range(2):
                        acc[ib * 8 + i + e] = y[:, e * 128 : e * 128 + 128]
                elif p == 1:
                    y = dot(wt[128:256, :], w)
                    for e in range(2):
                        acc[ib * 8 + i + e] = acc[ib * 8 + i + e] + y[:, e * 128 : e * 128 + 128]
                else:
                    y = dot(wt[...], w)
                    for e in range(2):
                        at = ib * 8 + i + e
                        scale = inv * rv_smem[gr * 48 + at].astype(F32)
                        ya = acc[at].T * scale + off_ref[...]
                        yb = (y[0:128, e * 128 : e * 128 + 128].T[0:64]
                              + y[128:256, e * 128 : e * 128 + 128].T[64:128])
                        yb = yb * scale + off_ref[...]
                        out_ref[at, pl.ds(off_a, 128), :] = ya.astype(BF16)
                        out_ref[at, pl.ds(off_b, 64), :] = yb.astype(BF16)


def vmem():
    return pl.BlockSpec(memory_space=pltpu.VMEM)


def smem():
    return pl.BlockSpec(memory_space=pltpu.SMEM)


def on_device(msa, sv, rv, gain, offset, w1, w2, wz, bz):
    dma = pltpu.SemaphoreType.DMA
    rg, lg = pl.pallas_call(
        comm_kernel,
        out_shape=(
            jax.ShapeDtypeStruct((16, 48, 32, 128), BF16),
            jax.ShapeDtypeStruct((16, 12, 32, 128), BF16),
        ),
        in_specs=[smem()] + [vmem()] * 6,
        out_specs=(vmem(), vmem()),
        scratch_shapes=[
            pltpu.VMEM((8, 3, 2, 16, 128), BF16),
            pltpu.VMEM((3, 16, 2, 16, 128), BF16),
            pltpu.VMEM((16, 48, 128), BF16),
            pltpu.VMEM((16, 48, 128), BF16),
            pltpu.VMEM((2, 12, 32, 128), BF16),
            pltpu.VMEM((1536, 128), F32),
            pltpu.VMEM((2, 384, 128), F32),
            pltpu.VMEM((16, 48, 128), F32),
            pltpu.VMEM((8, 128), F32),
            dma((3, 16)), dma((3, 16)),
            dma((16,)), dma((16,)),
            dma((8,)), dma((8,)),
            dma((8,)), dma((8,)),
            dma((3, 2, 20)), dma((3, 2, 20)),
        ],
        compiler_params=pltpu.CompilerParams(
            collective_id=0, has_side_effects=True, vmem_limit_bytes=40 * 2**20),
    )(sv, msa, rv.reshape(4, 1, 384), gain.reshape(1, 64), offset.reshape(1, 64), w1, w2)
    return pl.pallas_call(
        tile_kernel,
        out_shape=jax.ShapeDtypeStruct((48, 192, 128), BF16),
        in_specs=[smem()] + [vmem()] * 5,
        out_specs=vmem(),
        scratch_shapes=[
            pltpu.VMEM((1024, 128), F32),
            pltpu.VMEM((1024, 128), BF16),
            pltpu.VMEM((256, 512), BF16),
            pltpu.VMEM((1536, 512), BF16),
            pltpu.VMEM((8, 16, 32, 128), BF16),
            pltpu.VMEM((48, 128, 128), F32),
        ],
        compiler_params=pltpu.CompilerParams(vmem_limit_bytes=40 * 2**20),
        cost_estimate=pl.CostEstimate(flops=12 * 10**9, bytes_accessed=10**7, transcendentals=0),
    )(rv, sv.reshape(4, 128), rg, lg, wz, bz.reshape(1, 128))


def solution(mesh):
    in_specs = (P(("gr", "gc"), None, None), P(), P(), P(), P(), P(), P(), P(), P())
    out_specs = P("gr", "gc", None)
    return jax.shard_map(
        on_device, mesh=mesh, in_specs=in_specs, out_specs=out_specs, check_vma=False
    )
```

time: 412 us -> 97.4 us (0.24); the launches traced: 405 us -> 97 us
  waiting for transfers between devices: 185 us -> 0 us
  Pallas kernels: 0 us -> 88.3 us
  local copies, waits for them, and re-layouts: 88.7 us -> 8.62 us
  matrix products: 70 us -> 0 us
  blocking collectives: 40.5 us -> 0 us
  between operations: 13.6 us -> 0.04 us
  other arithmetic: 5.24 us -> 0 us
    all_gather x2 -> x0, waiting for transfers between devices: 185 us -> none  [the longest x1 160 us: on_device(): lax.all_gather(moved[:, per_device * hidden:], 'gr', axis=1, tiled=True)]
    pallas_call x0 -> x2, Pallas kernels: none -> 88.3 us  [the longest x1 60.9 us: on_device(): pl.pallas_call(comm_kernel, out_shape=(jax.ShapeDtypeStruct((16, 48, 32,...]
    reshape x7 -> x1, local copies, waits for them, and re-layouts: 75.1 us -> 0.71 us  [on_device(): rv.reshape(4, 1, 384)]
    dot_general x7 -> x0, matrix products: 70 us -> none  [the longest x3 44.1 us: one_block(): jnp.einsum('icjd,cdz->ijz', outer, weight3, preferred_element_type=jnp.fl...]
    all_to_all x2 -> x0, blocking collectives: 40.5 us -> none  [the longest x1 22.6 us: on_device(): lax.all_to_all(lax.all_to_all(packed, 'gr', split_axis=1, concat_axis=1,...]
    while x1 -> x0, local copies, waits for them, and re-layouts: 8.67 us -> none  [on_device(): result = lax.map(one_block, jnp.arange(nblocks, dtype=jnp.int32))]
    unnamed x6 -> x17, local copies, waits for them, and re-layouts: 0.02 us -> 7.92 us
  transfers between devices with their start and end apart: 2 -> 0, of which waited for: 2 -> 0; matrix products, arithmetic and copies ran while one was open for 1% -> 0% of each run, Pallas kernels for 0% -> 0%
where the time goes in v1:
time: 97.4 us; the launch traced here: 97 us
  Pallas kernels  88.3 us (91%)
  local copies, waits for them, and re-layouts  8.62 us (9%)
    pallas_call x1, Pallas kernels, on_device(): pl.pallas_call(comm_kernel, out_shape=(jax.ShapeDtypeStruct((16, 48, 32,...  60.9 us
    pallas_call x1, Pallas kernels, on_device(): pl.pallas_call(tile_kernel, out_shape=jax.ShapeDtypeStruct((48, 192, 128)...  27.4 us
    unnamed x17, local copies, waits for them, and re-layouts  7.92 us

profile of v1, /device:TPU:2, one launch (start us, length us, event | category | flops | bytes accessed | tf_op | source)
XLA Modules:
  0.0 97.0 jit_solution(3324395064701055242)
XLA Ops:
  0.0 0.7 reshape.16.rv_ref
  0.7 0.8 copy.11.w1_ref
  1.5 0.8 copy.12.w2_ref
  2.3 1.4 %copy.10.msa_ref = bf16[2,1536,64]{2,1,0:T(8,128)(2,1)S(1)} copy(bf16[2,1536,64]{1,2,0:T(8,128)(2,1)} %param.9) | data formatting | bytes 786432 | tf_op args[0]
  3.7 0.0 copy-start.1
  3.7 0.7 copy-done.1
  4.4 0.0 copy-start.3
  4.4 0.7 copy-done.3
  5.0 0.0 copy-start.4
  5.0 0.7 copy-done.4
  5.7 60.9 %shard_map.91 = (bf16[16,48,32,128]{3,2,1,0:T(8,128)(2,1)S(1)}, bf16[16,12,32,128]{3,2,1,0:T(8,128)(2,1)S(1)}) custom-call(s32[512]{0:T(512)S(1)} %copy-done.1, bf16[2,1536,64]{2,1,0:T(8,128)(2,1)S(1)} %copy.10.msa_ref, s32[4,1,384]{2,1,0:T(1,128)S(1)} %reshape.16.rv_ref, f32[1,64]{1,0:T(1,128)S(1)} %bitcast.5, f32[1,64]{1,0:T(1,128)S(1)} %bitcast.6, ...), custom_call_target="tpu_custom_call" | custom-call | tf_op jit(solution)/shard_map/pallas_call | solution.py:430
  66.6 0.0 copy-start
  66.6 0.7 copy-done
  67.3 0.0 copy-start.2
  67.3 0.7 copy-done.2
  67.9 0.0 copy-start.5
  68.0 0.9 copy-done.5
  68.9 0.0 copy-start.6
  68.9 0.7 copy-done.6
  69.6 27.4 %shard_map.92 = bf16[48,192,128]{2,1,0:T(8,128)(2,1)} custom-call(s32[1536]{0:T(1024)S(1)} %copy-done, s32[4,128]{1,0:T(4,128)S(1)} %bitcast.4, bf16[16,48,32,128]{3,2,1,0:T(8,128)(2,1)S(1)} %get-tuple-element.7.rg, bf16[16,12,32,128]{3,2,1,0:T(8,128)(2,1)S(1)} %get-tuple-element.8.lg, bf16[1024,128]{1,0:T(8,128)(2,1)S(1)} %copy-done.5, f32[1,128]{1,0:T(1,128)S(1)} %bitcast.7), custom_call_target="tpu_custom_call" | custom-call | flops 12000000000 | bytes 10000000 | tf_op jit(solution)/shard_map/pallas_call | solution.py:457
Async XLA Ops:
  3.7 0.7 copy-start.1
  4.4 0.7 copy-start.3
  5.0 0.7 copy-start.4
  66.6 0.7 copy-start
  67.3 0.7 copy-start.2
  67.9 0.9 copy-start.5
  68.9 0.7 copy-start.6

commit v2 on v0

v2 whole, which is shorter than its diff:
```python
import functools
import jax
import jax.numpy as jnp
from jax import lax
from jax.experimental import pallas as pl
from jax.experimental.pallas import tpu as pltpu
from jax.sharding import PartitionSpec as P

F32 = jnp.float32
BF16 = jnp.bfloat16
MESH = pl.DeviceIdType.MESH
NT = (((1,), (1,)), ((), ()))


def iota(shape, dim):
    return lax.broadcasted_iota(jnp.int32, shape, dim)


def ones_where(cond):
    return jnp.where(cond, 1.0, 0.0).astype(BF16)


def dot(a, b):
    return jnp.dot(a, b, preferred_element_type=F32)


def dot_nt(a, b):
    return lax.dot_general(a, b, NT, preferred_element_type=F32)


def where_am_i():
    gr = lax.axis_index("gr")
    gc = lax.axis_index("gc")
    zl = gr // 16
    pos = gr % 16
    zc = ((gc // 2) * 2 + zl) * 2 + gc % 2
    return gr, gc, zl, pos, zc


def ring_device(zl_to_gr, zc):
    z = zc // 2
    return {"gr": (z % 2) * 16 + zl_to_gr, "gc": (z // 2) * 2 + zc % 2}


def plane_device(zl, gc, pos):
    return {"gr": zl * 16 + pos, "gc": gc}


PIECES = (32, 40, 0, 8, 16, 24)
TILES = 8


def first_product(lt, rg, outer, ib, t0):
    x = lt[pl.ds(pl.multiple_of(ib * 512, 512), 512), :]
    for t in range(0, TILES, 2):
        w = jnp.concatenate([rg[:, t0 + t + e].reshape(512, 128) for e in range(2)], axis=1)
        s = dot(x, w).astype(BF16)
        for i in range(16):
            for e in range(2):
                outer[i, t + e] = s[i * 32 : i * 32 + 32, e * 128 : e * 128 + 128]


def second_product(w, outer, i):
    return dot(w, jnp.concatenate([outer[i + e].reshape(TILES * 32, 128) for e in range(2)], axis=1))


def main_kernel(
    sv_hbm, sv4_hbm, rv_hbm, rv12_hbm, msa_hbm, gain_hbm, off_hbm, w1_hbm, w2_hbm, wz_hbm, bz_hbm,
    out_hbm,
    rg, lt, acc, accb, outv, scale, wt, bz,
    sv_smem, rv_smem, sv4, rv12, msa, gain1, off1, w1, w2, wz,
    rs, rb, ls, la, lb, lg, n2, x4, lq, lsf, gainv, fpf, wd, outer,
    in_sem, out_sem, rs_send, rs_recv, ls_send, ls_recv, lz_send, lz_recv, lt_send, lt_recv,
    g_send, g_recv,
):
    gr, gc, zl, pos, zc = where_am_i()
    core = gc % 2
    px, py = pos // 4, pos % 4
    twin = {"gr": gr, "gc": gc + 1 - 2 * core}

    moves = [
        pltpu.make_async_copy(src, dst, in_sem.at[i])
        for i, (src, dst) in enumerate((
            (msa_hbm, msa), (gain_hbm, gain1), (off_hbm, off1), (w2_hbm, w2), (rv12_hbm, rv12), (sv_hbm, sv_smem),
            (w1_hbm, w1), (sv4_hbm, sv4), (rv_hbm, rv_smem), (wz_hbm, wz), (bz_hbm, bz)))
    ]
    for m in moves:
        m.start()

    barrier = pltpu.get_barrier_semaphore()

    @pl.loop(1, 16)
    def _(o):
        pl.semaphore_signal(barrier, inc=1, device_id=ring_device(pos, (zc + o) % 16), device_id_type=MESH)
        pl.semaphore_signal(barrier, inc=1, device_id=plane_device(zl, gc, (pos + o) % 16), device_id_type=MESH)

    for m in moves[:6]:
        m.wait()

    gainv[0:1, 0:64] = gain1[...]
    gainv[0:1, 64:128] = gain1[...]
    gainv[1:2, 0:64] = off1[...]
    gainv[1:2, 64:128] = off1[...]
    gcol = jnp.broadcast_to(gainv[0:1, :], (128, 128)).T[0:64]
    ocol = jnp.broadcast_to(gainv[1:2, :], (128, 128)).T[0:64]
    gcol = jnp.concatenate([gcol] * 3, axis=1)
    ocol = jnp.concatenate([ocol] * 3, axis=1)
    low = iota((16, 128), 1) < 64
    for g in range(4):
        present = jnp.concatenate([rv12[3 * g + k : 3 * g + k + 1, :] for k in range(3)], axis=1).astype(F32)
        for r in range(2):
            x = msa[r, :, 384 * g : 384 * g + 384].astype(F32)
            d = x - jnp.mean(x, axis=0, keepdims=True)
            var = jnp.mean(d * d, axis=0, keepdims=True)
            n = (d * lax.rsqrt(var + 1e-05) * gcol + ocol).astype(BF16)
            n2[r * 64 : r * 64 + 64, 384 * g : 384 * g + 384] = n
            yr = dot(w2[...], n) * (present * sv_smem[(gr * 8 + gc) * 2 + r].astype(F32))
            a, b = yr[0:16, 128:256], yr[16:32, 128:256]
            rs[2 * g, 0, r] = jnp.where(low, a, pltpu.roll(b, 64, axis=1)).astype(BF16)
            rs[2 * g, 1, r] = yr[0:16, 0:128].astype(BF16)
            rs[2 * g, 2, r] = yr[16:32, 0:128].astype(BF16)
            rs[2 * g + 1, 0, r] = jnp.where(low, pltpu.roll(a, 64, axis=1), b).astype(BF16)
            rs[2 * g + 1, 1, r] = yr[0:16, 256:384].astype(BF16)
            rs[2 * g + 1, 2, r] = yr[16:32, 256:384].astype(BF16)

    pl.semaphore_wait(barrier, 30)

    def wait_bytes(ref, sem):
        pltpu.make_async_copy(ref, ref, sem).wait()

    def rs_start(first, n):
        part = pl.ds(first, n)

        @pl.loop(1, 16)
        def _(o):
            to = ring_device(pos, (zc + o) % 16)
            pltpu.make_async_remote_copy(
                src_ref=rs.at[to["gc"], part], dst_ref=rb.at[part, zc],
                send_sem=rs_send, recv_sem=rs_recv.at[first],
                device_id=to, device_id_type=MESH).start()

        for p in range(first, first + n):
            rb[p, zc] = rs[gc, p]

    rs_start(0, 1)
    rs_start(1, 2)

    for m in moves[6:]:
        m.wait()
    sel = ones_where((iota((128, 128), 0) % 32) * 4 + iota((128, 128), 0) // 32 == iota((128, 128), 1))
    for k in range(12):
        t = dot_nt(sel, n2[:, 128 * k : 128 * k + 128]).astype(BF16)
        for m in range(4):
            x4[32 * k : 32 * k + 32, 128 * m : 128 * m + 128] = t[32 * m : 32 * m + 32]
    t1 = ones_where(iota((512, 64), 0) % 64 == iota((512, 64), 1))
    t2 = ones_where(iota((32, 256), 1) % 32 == iota((32, 256), 0))
    row, col = iota((512, 256), 0), iota((512, 256), 1)
    wl = dot(dot_nt(t1, w1[...]).astype(BF16), t2)
    wl = jnp.where((row // 128 == (col // 32) % 4) & ((row // 64) % 2 == col // 128), wl, 0.0).astype(BF16)
    left = dot(x4[...], wl)
    lq[0] = left[:, 0:128]
    lq[1] = left[:, 128:256]
    for p in range(16):
        for l in range(2):
            for r in range(2):
                at = 12 * (l * 16 + p)
                lsf[p, l * 24 + r * 12 : l * 24 + r * 12 + 12, :] = lq[r, at : at + 12, :]
    ls[...] = lsf[...].astype(BF16)

    @pl.loop(1, 16)
    def _(o):
        to = (pos + o) % 16
        pltpu.make_async_remote_copy(
            src_ref=ls.at[to], dst_ref=la.at[pos],
            send_sem=ls_send, recv_sem=ls_recv,
            device_id=plane_device(zl, gc, to), device_id_type=MESH).start()

    la[pos] = ls[pos]

    def flat(x, y):
        return ((x + 4) % 4) * 4 + (y + 4) % 4

    def along(half, a, b):
        return flat(px + a, py + b) if half == 0 else flat(px + b, py + a)

    def g_send_to(k, half, level, who, part, da, db):
        t0, unit = PIECES[k], TILES // 2
        u0, un = {"all": (0, unit), "lo": (0, unit // 2), "hi": (unit // 2, unit // 2)}[part]
        t = pl.ds(t0 + unit * half + u0, un)
        pltpu.make_async_remote_copy(
            src_ref=rg.at[who, t], dst_ref=rg.at[who, t],
            send_sem=g_send, recv_sem=g_recv.at[k, level - 1],
            device_id=plane_device(zl, gc, along(half, da, db)), device_id_type=MESH).start()

    def both_ways(k, level, u):
        for h in range(2):
            g_send_to(k, h, level, along(h, u, 0), "all", 0, 1)
            g_send_to(k, h, level, along(h, u, 0), "all", 0, -1)

    def forward(k, u):
        for h in range(2):
            g_send_to(k, h, 4, along(h, u, -1), "lo", 0, 1)
            g_send_to(k, h, 4, along(h, u, 1), "hi", 0, -1)

    def level0(k):
        for h in range(2):
            g_send_to(k, h, 1, along(h, 0, 0), "all", 1, 0)
            g_send_to(k, h, 1, along(h, 0, 0), "all", -1, 0)
        both_ways(k, 1, 0)

    def level1(k):
        wait_bytes(rg.at[0:8, 0 : TILES // 2], g_recv.at[k, 0])
        for h in range(2):
            g_send_to(k, h, 2, along(h, -1, 0), "lo", 1, 0)
            g_send_to(k, h, 2, along(h, 1, 0), "hi", -1, 0)
        both_ways(k, 2, 3)
        both_ways(k, 2, 1)
        forward(k, 0)

    def level2(k):
        wait_bytes(rg.at[0:10, 0 : TILES // 2], g_recv.at[k, 1])
        both_ways(k, 3, 2)
        forward(k, 3)
        forward(k, 1)

    def level3(k):
        wait_bytes(rg.at[0:4, 0 : TILES // 2], g_recv.at[k, 2])
        forward(k, 2)

    def level4(k):
        wait_bytes(rg.at[0:8, 0 : TILES // 2], g_recv.at[k, 3])

    levels = (level0, level1, level2, level3, level4)

    def wave(i):
        for d in range(4, -1, -1):
            for k, first in enumerate((0, 0, 1, 2, 3, 4)):
                if first + d == i:
                    levels[d](k)

    o0, i0 = iota((512, 1), 0), iota((512, 512), 1)
    perm0 = ones_where((o0 % 32) * 16 + o0 // 32 == i0)

    def assemble_right(p):
        x = rb[p].reshape(512, 128)
        t0 = (32, 0, 16)[p]
        rg[pos, t0 : t0 + 16] = dot(perm0, x).astype(BF16).reshape(16, 32, 128)

    def assemble_left():
        o1, i1 = iota((768, 1), 0), iota((768, 768), 1)
        lq1 = o1 // 32
        l1 = jnp.where(lq1 >= 12, 1, 0)
        at = ((o1 // 2) % 16) * 48 + l1 * 24 + (o1 % 2) * 12 + (lq1 - 12 * l1)
        perm1 = ones_where(at == i1)

        wait_bytes(la.at[0:15], ls_recv)
        y = dot(perm1, la[...].reshape(768, 128)).astype(BF16)
        lb[...] = y.reshape(2, 12, 32, 128)
        lg[zc] = lb[zl]

    def at_z(d):
        return (zc + 2 * d + 16) % 16

    def lz(level, src, slot, to, part):
        t = pl.ds(*{"all": (0, 12), "lo": (0, 6), "hi": (6, 6)}[part])
        pltpu.make_async_remote_copy(
            src_ref=src.at[t], dst_ref=lg.at[slot, t],
            send_sem=lz_send, recv_sem=lz_recv.at[level],
            device_id=ring_device(pos, at_z(to)), device_id_type=MESH).start()

    def twin_send(d):
        pltpu.make_async_remote_copy(
            src_ref=lg.at[at_z(d)], dst_ref=lg.at[at_z(d)],
            send_sem=lt_send, recv_sem=lt_recv,
            device_id=twin, device_id_type=MESH).start()

    def lz_start():
        for d in (1, -1):
            lz(0, lb.at[1 - zl], zc, d, "all")
        for d in (2, -2):
            lz(0, lb.at[zl], zc, d, "all")
        twin_send(0)

    def lz_forward():
        wait_bytes(lg.at[0:4], lz_recv.at[0])
        for d in (1, -1):
            lz(1, lg.at[at_z(-d)], at_z(-d), 2 * d, "all")
        lz(1, lg.at[at_z(-2)], at_z(-2), 2, "lo")
        lz(1, lg.at[at_z(2)], at_z(2), -2, "hi")
        for d in (-1, 1, -2, 2):
            twin_send(d)

    def lz_end():
        wait_bytes(lg.at[0:3], lz_recv.at[1])
        for d in (-3, 3, 4):
            twin_send(d)

    eye = ones_where(iota((128, 128), 0) == iota((128, 128), 1))

    def weights():
        fpf[...] = wz[...].astype(F32)
        for d in range(32):
            wd[32 * d : 32 * d + 32, :] = fpf[pl.ds(d, 32, stride=32), :].astype(BF16)
        wfull = dot_nt(eye, wd[...]).astype(BF16)
        wt[0:128, :] = wfull[:, 0:512]
        wt[128:256, :] = wfull[:, 512:1024]
        count = jnp.sum(sv4[...].astype(F32))
        inv = 1.0 / jnp.full((1, 128), count, F32)
        for i in range(48):
            scale[i : i + 1, :] = inv * rv_smem[gr * 48 + i].astype(F32)

    def turn_left():
        wait_bytes(lg.at[0:8], lt_recv)
        o2, i2 = iota((512, 1), 0), iota((512, 512), 1)
        perm2 = ones_where(((o2 // 2) % 16) * 32 + (o2 // 32) * 2 + o2 % 2 == i2)
        for b in range(3):
            x = jnp.concatenate([lg[:, 4 * b + e].reshape(512, 128).T for e in range(4)], axis=0)
            lt[512 * b : 512 * b + 512, :] = dot_nt(x, perm2).astype(BF16)

    half_lanes = iota((128, 128), 1) < 64

    off_a = pl.multiple_of(64 * core, 64)
    off_b = pl.multiple_of(128 - 128 * core, 64)

    def move_out(ib):
        rows = pl.ds(ib * 16, 16)
        return pltpu.make_async_copy(outv.at[rows], out_hbm.at[rows], out_sem.at[ib])

    def compute(k):
        t0 = PIECES[k]

        @pl.loop(0, 3)
        def _(ib):
            first_product(lt, rg, outer, ib, t0)
            at = t0 % 16 * 32
            if k < 2:
                w = wt[:, at : at + 256]
            else:
                w = wt[t0 // 16 * 128 : t0 // 16 * 128 + 128, at : at + 256]
            for i in range(0, 16, 2):
                y2 = second_product(w, outer, i)
                for e in range(2):
                    me = ib * 16 + i + e
                    y = y2[:, e * 128 : e * 128 + 128]
                    if k < 2:
                        y = jnp.where(half_lanes, y[0:128], y[128:256])
                    if k == 0:
                        accb[me] = y
                    elif k == 1:
                        y = (accb[me] + y).T
                        y = (y[0:64] + y[64:128]) * scale[pl.ds(me, 1), :] + bz[...]
                        outv[me, pl.ds(off_b, 64), :] = y.astype(BF16)
                    elif k == 2:
                        acc[me] = y
                    elif k < 5:
                        acc[me] = acc[me] + y
                    else:
                        y = (acc[me] + y).T * scale[pl.ds(me, 1), :] + bz[...]
                        outv[me, pl.ds(off_a, 128), :] = y.astype(BF16)
            if k == 5:
                move_out(ib).start()

    wait_bytes(rb.at[0, 0:15], rs_recv.at[0])
    assemble_right(0)
    wave(0)
    assemble_left()
    lz_start()
    wait_bytes(rb.at[1:3, 0:15], rs_recv.at[1])
    assemble_right(1)
    assemble_right(2)
    wave(1)
    wave(2)
    weights()
    wave(3)
    lz_forward()
    wave(4)
    lz_end()
    turn_left()
    compute(0)
    wave(5)
    compute(1)
    compute(2)
    wave(6)
    compute(3)
    wave(7)
    compute(4)
    wave(8)
    compute(5)

    wait_bytes(rg.at[0:15], g_send)
    wait_bytes(rb.at[:, 0:15], rs_send)
    wait_bytes(la.at[0:15], ls_send)
    wait_bytes(lg.at[0:7], lz_send)
    wait_bytes(lg.at[0:8], lt_send)

    @pl.loop(0, 3)
    def _(ib):
        move_out(ib).wait()


def hbm():
    return pl.BlockSpec(memory_space=pltpu.HBM)


def on_device(msa, sv, rv, gain, offset, w1, w2, wz, bz):
    dma = pltpu.SemaphoreType.DMA
    i32 = jnp.int32
    return pl.pallas_call(
        main_kernel,
        name="gather_and_compute",
        out_shape=jax.ShapeDtypeStruct((48, 192, 128), BF16),
        in_specs=[hbm()] * 11,
        out_specs=hbm(),
        scratch_shapes=[
            pltpu.VMEM((16, 48, 32, 128), BF16),
            pltpu.VMEM((1536, 512), BF16),
            pltpu.VMEM((48, 128, 128), F32),
            pltpu.VMEM((48, 128, 128), F32),
            pltpu.VMEM((48, 192, 128), BF16),
            pltpu.VMEM((48, 128), F32),
            pltpu.VMEM((256, 512), BF16),
            pltpu.VMEM((1, 128), F32),
            pltpu.SMEM((512,), i32),
            pltpu.SMEM((1536,), i32),
            pltpu.VMEM((4, 128), i32),
            pltpu.VMEM((12, 128), i32),
            pltpu.VMEM((2, 64, 1536), BF16),
            pltpu.VMEM((1, 64), F32),
            pltpu.VMEM((1, 64), F32),
            pltpu.VMEM((32, 64), BF16),
            pltpu.VMEM((32, 64), BF16),
            pltpu.VMEM((1024, 128), BF16),
            pltpu.VMEM((8, 3, 2, 16, 128), BF16),
            pltpu.VMEM((3, 16, 2, 16, 128), BF16),
            pltpu.VMEM((16, 48, 128), BF16),
            pltpu.VMEM((16, 48, 128), BF16),
            pltpu.VMEM((2, 12, 32, 128), BF16),
            pltpu.VMEM((16, 12, 32, 128), BF16),
            pltpu.VMEM((128, 1536), BF16),
            pltpu.VMEM((384, 512), BF16),
            pltpu.VMEM((2, 384, 128), F32),
            pltpu.VMEM((16, 48, 128), F32),
            pltpu.VMEM((8, 128), F32),
            pltpu.VMEM((1024, 128), F32),
            pltpu.VMEM((1024, 128), BF16),
            pltpu.VMEM((16, TILES, 32, 128), BF16),
            dma((11,)),
            dma((3,)),
            dma, dma((2,)),
            dma, dma,
            dma, dma((2,)),
            dma, dma,
            dma, dma((len(PIECES), 4)),
        ],
        compiler_params=pltpu.CompilerParams(
            collective_id=0, has_side_effects=True, vmem_limit_bytes=56 * 2**20),
    )(sv, sv.reshape(4, 128), rv, rv.reshape(12, 128), msa.transpose(0, 2, 1), gain.reshape(1, 64),
      offset.reshape(1, 64), w1.T, w2.T, wz, bz.reshape(1, 128))


def solution(mesh):
    in_specs = (P(("gr", "gc"), None, None), P(), P(), P(), P(), P(), P(), P(), P())
    out_specs = P("gr", "gc", None)
    return jax.shard_map(
        on_device, mesh=mesh, in_specs=in_specs, out_specs=out_specs, check_vma=False
    )
```

time: 412 us -> 72.1 us (0.17)
  the two profiles are of different devices: /device:TPU:2 before, /device:TPU:1 now
where the time goes in v2:
time: 72.1 us; the launch traced here: 72 us
  Pallas kernels  68.8 us (95%)
  local copies, waits for them, and re-layouts  3.22 us (4%)
    pallas_call x1, Pallas kernels, on_device(): pl.pallas_call(main_kernel, name='gather_and_compute', out_shape=jax.Shap...  68.8 us
    unnamed x1, local copies, waits for them, and re-layouts  3.22 us

profile of v2, /device:TPU:1, one launch (start us, length us, event | category | flops | bytes accessed | tf_op | source)
XLA Modules:
  0.0 72.0 jit_solution(553931007452647054)
XLA Ops:
  0.0 68.8 %gather_and_compute.1 = bf16[48,192,128]{2,1,0:T(8,128)(2,1)} custom-call(s32[512]{0:T(512)} %sv_hbm.1, s32[4,128]{1,0:T(4,128)} %bitcast.12, s32[1536]{0:T(1024)} %rv_hbm.1, s32[12,128]{1,0:T(8,128)} %bitcast.9, bf16[2,64,1536]{2,1,0:T(8,128)(2,1)} %bitcast.8, f32[1,64]{1,0:T(1,128)} %bitcast.13, f32[1,64]{1,0:T(1,128)} %bitcast.14, ...), custom_call_target="tpu_custom_call" | custom-call | tf_op jit(solution)/shard_map/gather_and_compute/pallas_call | solution.py:408
  68.8 3.2 %copy.11 = bf16[48,192,128]{2,1,0:T(8,128)(2,1)} copy(bf16[48,192,128]{2,1,0:T(8,128)(2,1)} %gather_and_compute.1) | data formatting | bytes 4718592

commit v3 on v2

--- a/solution.py
+++ b/solution.py
@@ -46,13 +46,12 @@
     return {"gr": zl * 16 + pos, "gc": gc}
 
 
-PIECES = (32, 40, 0, 8, 16, 24)
-TILES = 8
-
-
-def first_product(lt, rg, outer, ib, t0):
+PIECES = ((32, 16), (0, 16), (16, 8), (24, 8))
+
+
+def first_product(lt, rg, outer, ib, t0, n):
     x = lt[pl.ds(pl.multiple_of(ib * 512, 512), 512), :]
-    for t in range(0, TILES, 2):
+    for t in range(0, n, 2):
         w = jnp.concatenate([rg[:, t0 + t + e].reshape(512, 128) for e in range(2)], axis=1)
         s = dot(x, w).astype(BF16)
         for i in range(16):
@@ -60,14 +59,14 @@
                 outer[i, t + e] = s[i * 32 : i * 32 + 32, e * 128 : e * 128 + 128]
 
 
-def second_product(w, outer, i):
-    return dot(w, jnp.concatenate([outer[i + e].reshape(TILES * 32, 128) for e in range(2)], axis=1))
+def second_product(w, outer, i, n):
+    return dot(w, jnp.concatenate([outer[i + e, 0:n].reshape(n * 32, 128) for e in range(2)], axis=1))
 
 
 def main_kernel(
     sv_hbm, sv4_hbm, rv_hbm, rv12_hbm, msa_hbm, gain_hbm, off_hbm, w1_hbm, w2_hbm, wz_hbm, bz_hbm,
     out_hbm,
-    rg, lt, acc, accb, outv, scale, wt, bz,
+    rg, lt, acc, outv, scale, wt, bz,
     sv_smem, rv_smem, sv4, rv12, msa, gain1, off1, w1, w2, wz,
     rs, rb, ls, la, lb, lg, n2, x4, lq, lsf, gainv, fpf, wd, outer,
     in_sem, out_sem, rs_send, rs_recv, ls_send, ls_recv, lz_send, lz_recv, lt_send, lt_recv,
@@ -128,22 +127,19 @@
     def wait_bytes(ref, sem):
         pltpu.make_async_copy(ref, ref, sem).wait()
 
-    def rs_start(first, n):
-        part = pl.ds(first, n)
-
+    def rs_start(p):
         @pl.loop(1, 16)
         def _(o):
             to = ring_device(pos, (zc + o) % 16)
             pltpu.make_async_remote_copy(
-                src_ref=rs.at[to["gc"], part], dst_ref=rb.at[part, zc],
-                send_sem=rs_send, recv_sem=rs_recv.at[first],
+                src_ref=rs.at[to["gc"], p], dst_ref=rb.at[p, zc],
+                send_sem=rs_send, recv_sem=rs_recv.at[p],
                 device_id=to, device_id_type=MESH).start()
 
-        for p in range(first, first + n):
-            rb[p, zc] = rs[gc, p]
-
-    rs_start(0, 1)
-    rs_start(1, 2)
+        rb[p, zc] = rs[gc, p]
+
+    rs_start(0)
+    rs_start(1)
 
     for m in moves[6:]:
         m.wait()
@@ -184,8 +180,9 @@
         return flat(px + a, py + b) if half == 0 else flat(px + b, py + a)
 
     def g_send_to(k, half, level, who, part, da, db):
-        t0, unit = PIECES[k], TILES // 2
-        u0, un = {"all": (0, unit), "lo": (0, unit // 2), "hi": (unit // 2, unit // 2)}[part]
+        t0, n = PIECES[k]
+        unit = n // 2
+        u0, un = {"both": (0, n), "all": (0, unit), "lo": (0, unit // 2), "hi": (unit // 2, unit // 2)}[part]
         t = pl.ds(t0 + unit * half + u0, un)
         pltpu.make_async_remote_copy(
             src_ref=rg.at[who, t], dst_ref=rg.at[who, t],
@@ -203,13 +200,11 @@
             g_send_to(k, h, 4, along(h, u, 1), "hi", 0, -1)
 
     def level0(k):
-        for h in range(2):
-            g_send_to(k, h, 1, along(h, 0, 0), "all", 1, 0)
-            g_send_to(k, h, 1, along(h, 0, 0), "all", -1, 0)
-        both_ways(k, 1, 0)
+        for da, db in ((1, 0), (-1, 0), (0, 1), (0, -1)):
+            g_send_to(k, 0, 1, pos, "both", da, db)
 
     def level1(k):
-        wait_bytes(rg.at[0:8, 0 : TILES // 2], g_recv.at[k, 0])
+        wait_bytes(rg.at[0:8, 0 : PIECES[k][1] // 2], g_recv.at[k, 0])
         for h in range(2):
             g_send_to(k, h, 2, along(h, -1, 0), "lo", 1, 0)
             g_send_to(k, h, 2, along(h, 1, 0), "hi", -1, 0)
@@ -218,30 +213,23 @@
         forward(k, 0)
 
     def level2(k):
-        wait_bytes(rg.at[0:10, 0 : TILES // 2], g_recv.at[k, 1])
+        wait_bytes(rg.at[0:10, 0 : PIECES[k][1] // 2], g_recv.at[k, 1])
         both_ways(k, 3, 2)
         forward(k, 3)
         forward(k, 1)
 
     def level3(k):
-        wait_bytes(rg.at[0:4, 0 : TILES // 2], g_recv.at[k, 2])
+        wait_bytes(rg.at[0:4, 0 : PIECES[k][1] // 2], g_recv.at[k, 2])
         forward(k, 2)
 
     def level4(k):
-        wait_bytes(rg.at[0:8, 0 : TILES // 2], g_recv.at[k, 3])
-
-    levels = (level0, level1, level2, level3, level4)
-
-    def wave(i):
-        for d in range(4, -1, -1):
-            for k, first in enumerate((0, 0, 1, 2, 3, 4)):
-                if first + d == i:
-                    levels[d](k)
+        wait_bytes(rg.at[0:8, 0 : PIECES[k][1] // 2], g_recv.at[k, 3])
 
     o0, i0 = iota((512, 1), 0), iota((512, 512), 1)
     perm0 = ones_where((o0 % 32) * 16 + o0 // 32 == i0)
 
     def assemble_right(p):
+        wait_bytes(rb.at[p, 0:15], rs_recv.at[p])
         x = rb[p].reshape(512, 128)
         t0 = (32, 0, 16)[p]
         rg[pos, t0 : t0 + 16] = dot(perm0, x).astype(BF16).reshape(16, 32, 128)
@@ -326,66 +314,68 @@
         rows = pl.ds(ib * 16, 16)
         return pltpu.make_async_copy(outv.at[rows], out_hbm.at[rows], out_sem.at[ib])
 
-    def compute(k):
-        t0 = PIECES[k]
+    def compute(k, steps):
+        t0, n = PIECES[k]
 
         @pl.loop(0, 3)
         def _(ib):
-            first_product(lt, rg, outer, ib, t0)
-            at = t0 % 16 * 32
-            if k < 2:
-                w = wt[:, at : at + 256]
+            for at, do in steps.items():
+                pl.when(ib == at)(do)
+            first_product(lt, rg, outer, ib, t0, n)
+            if k == 0:
+                w = wt[...]
             else:
-                w = wt[t0 // 16 * 128 : t0 // 16 * 128 + 128, at : at + 256]
+                at = t0 % 16 * 32
+                w = wt[t0 // 16 * 128 : t0 // 16 * 128 + 128, at : at + n * 32]
             for i in range(0, 16, 2):
-                y2 = second_product(w, outer, i)
+                y2 = second_product(w, outer, i, n)
                 for e in range(2):
                     me = ib * 16 + i + e
                     y = y2[:, e * 128 : e * 128 + 128]
-                    if k < 2:
-                        y = jnp.where(half_lanes, y[0:128], y[128:256])
                     if k == 0:
-                        accb[me] = y
-                    elif k == 1:
-                        y = (accb[me] + y).T
+                        y = jnp.where(half_lanes, y[0:128], y[128:256]).T
                         y = (y[0:64] + y[64:128]) * scale[pl.ds(me, 1), :] + bz[...]
                         outv[me, pl.ds(off_b, 64), :] = y.astype(BF16)
-                    elif k == 2:
+                    elif k == 1:
                         acc[me] = y
-                    elif k < 5:
+                    elif k < 3:
                         acc[me] = acc[me] + y
                     else:
                         y = (acc[me] + y).T * scale[pl.ds(me, 1), :] + bz[...]
                         outv[me, pl.ds(off_a, 128), :] = y.astype(BF16)
-            if k == 5:
+            if k == 3:
                 move_out(ib).start()
 
-    wait_bytes(rb.at[0, 0:15], rs_recv.at[0])
     assemble_right(0)
-    wave(0)
+    level0(0)
     assemble_left()
     lz_start()
-    wait_bytes(rb.at[1:3, 0:15], rs_recv.at[1])
+    rs_start(2)
     assemble_right(1)
+    level0(1)
+    level1(0)
+    weights()
+    level1(1)
+    level2(0)
+    lz_forward()
+    level3(0)
     assemble_right(2)
-    wave(1)
-    wave(2)
-    weights()
-    wave(3)
-    lz_forward()
-    wave(4)
+    level0(2)
+    level0(3)
+    level2(1)
+    level1(2)
     lz_end()
+    level4(0)
     turn_left()
-    compute(0)
-    wave(5)
-    compute(1)
-    compute(2)
-    wave(6)
-    compute(3)
-    wave(7)
-    compute(4)
-    wave(8)
-    compute(5)
+    level3(1)
+    compute(0, {1: lambda: level1(3), 2: lambda: level2(2)})
+    level4(1)
+    level2(3)
+    compute(1, {1: lambda: level3(2), 2: lambda: level3(3)})
+    level4(2)
+    compute(2, {})
+    level4(3)
+    compute(3, {})
 
     wait_bytes(rg.at[0:15], g_send)
     wait_bytes(rb.at[:, 0:15], rs_send)
@@ -414,7 +404,6 @@
         scratch_shapes=[
             pltpu.VMEM((16, 48, 32, 128), BF16),
             pltpu.VMEM((1536, 512), BF16),
-            pltpu.VMEM((48, 128, 128), F32),
             pltpu.VMEM((48, 128, 128), F32),
             pltpu.VMEM((48, 192, 128), BF16),
             pltpu.VMEM((48, 128), F32),
@@ -443,10 +432,10 @@
             pltpu.VMEM((8, 128), F32),
             pltpu.VMEM((1024, 128), F32),
             pltpu.VMEM((1024, 128), BF16),
-            pltpu.VMEM((16, TILES, 32, 128), BF16),
+            pltpu.VMEM((16, 16, 32, 128), BF16),
             dma((11,)),
             dma((3,)),
-            dma, dma((2,)),
+            dma, dma((3,)),
             dma, dma,
             dma, dma((2,)),
             dma, dma,

time: 72.1 us -> 66.4 us (0.921)
  the two profiles are of different devices: /device:TPU:1 before, /device:TPU:2 now
where the time goes in v3:
time: 66.4 us; the launch traced here: 65.1 us
  Pallas kernels  61.8 us (93%)
  local copies, waits for them, and re-layouts  3.22 us (5%)
    pallas_call x1, Pallas kernels, on_device(): pl.pallas_call(main_kernel, name='gather_and_compute', out_shape=jax.Shap...  61.8 us
    unnamed x1, local copies, waits for them, and re-layouts  3.22 us

profile of v3, /device:TPU:2, one launch (start us, length us, event | category | flops | bytes accessed | tf_op | source)
XLA Modules:
  0.0 65.1 jit_solution(8069434048292871839)
XLA Ops:
  0.0 61.8 %gather_and_compute.1 = bf16[48,192,128]{2,1,0:T(8,128)(2,1)} custom-call(s32[512]{0:T(512)} %sv_hbm.1, s32[4,128]{1,0:T(4,128)} %bitcast.12, s32[1536]{0:T(1024)} %rv_hbm.1, s32[12,128]{1,0:T(8,128)} %bitcast.9, bf16[2,64,1536]{2,1,0:T(8,128)(2,1)} %bitcast.8, f32[1,64]{1,0:T(1,128)} %bitcast.13, f32[1,64]{1,0:T(1,128)} %bitcast.14, ...), custom_call_target="tpu_custom_call" | custom-call | tf_op jit(solution)/shard_map/gather_and_compute/pallas_call | solution.py:398
  61.9 3.2 %copy.11 = bf16[48,192,128]{2,1,0:T(8,128)(2,1)} copy(bf16[48,192,128]{2,1,0:T(8,128)(2,1)} %gather_and_compute.1) | data formatting | bytes 4718592

commit v4 on v3

--- a/solution.py
+++ b/solution.py
@@ -46,15 +46,16 @@
     return {"gr": zl * 16 + pos, "gc": gc}
 
 
+ROWS = 24
 PIECES = ((32, 16), (0, 16), (16, 8), (24, 8))
 
 
 def first_product(lt, rg, outer, ib, t0, n):
-    x = lt[pl.ds(pl.multiple_of(ib * 512, 512), 512), :]
+    x = lt[pl.ds(pl.multiple_of(ib * ROWS * 32, ROWS * 32), ROWS * 32), :]
     for t in range(0, n, 2):
         w = jnp.concatenate([rg[:, t0 + t + e].reshape(512, 128) for e in range(2)], axis=1)
         s = dot(x, w).astype(BF16)
-        for i in range(16):
+        for i in range(ROWS):
             for e in range(2):
                 outer[i, t + e] = s[i * 32 : i * 32 + 32, e * 128 : e * 128 + 128]
 
@@ -311,13 +312,13 @@
     off_b = pl.multiple_of(128 - 128 * core, 64)
 
     def move_out(ib):
-        rows = pl.ds(ib * 16, 16)
+        rows = pl.ds(ib * ROWS, ROWS)
         return pltpu.make_async_copy(outv.at[rows], out_hbm.at[rows], out_sem.at[ib])
 
     def compute(k, steps):
         t0, n = PIECES[k]
 
-        @pl.loop(0, 3)
+        @pl.loop(0, 48 // ROWS)
         def _(ib):
             for at, do in steps.items():
                 pl.when(ib == at)(do)
@@ -327,10 +328,10 @@
             else:
                 at = t0 % 16 * 32
                 w = wt[t0 // 16 * 128 : t0 // 16 * 128 + 128, at : at + n * 32]
-            for i in range(0, 16, 2):
+            for i in range(0, ROWS, 2):
                 y2 = second_product(w, outer, i, n)
                 for e in range(2):
-                    me = ib * 16 + i + e
+                    me = ib * ROWS + i + e
                     y = y2[:, e * 128 : e * 128 + 128]
                     if k == 0:
                         y = jnp.where(half_lanes, y[0:128], y[128:256]).T
@@ -349,29 +350,35 @@
     assemble_right(0)
     level0(0)
     assemble_left()
+    rs_start(2)
     lz_start()
-    rs_start(2)
     assemble_right(1)
     level0(1)
     level1(0)
     weights()
     level1(1)
     level2(0)
-    lz_forward()
-    level3(0)
     assemble_right(2)
     level0(2)
     level0(3)
+    lz_forward()
+    level3(0)
     level2(1)
     level1(2)
+    level1(3)
     lz_end()
     level4(0)
     turn_left()
     level3(1)
-    compute(0, {1: lambda: level1(3), 2: lambda: level2(2)})
+
+    def level2_both():
+        level2(2)
+        level2(3)
+
+    compute(0, {1: level2_both})
     level4(1)
-    level2(3)
-    compute(1, {1: lambda: level3(2), 2: lambda: level3(3)})
+    level3(2)
+    compute(1, {1: lambda: level3(3)})
     level4(2)
     compute(2, {})
     level4(3)
@@ -383,7 +390,7 @@
     wait_bytes(lg.at[0:7], lz_send)
     wait_bytes(lg.at[0:8], lt_send)
 
-    @pl.loop(0, 3)
+    @pl.loop(0, 48 // ROWS)
     def _(ib):
         move_out(ib).wait()
 
@@ -432,7 +439,7 @@
             pltpu.VMEM((8, 128), F32),
             pltpu.VMEM((1024, 128), F32),
             pltpu.VMEM((1024, 128), BF16),
-            pltpu.VMEM((16, 16, 32, 128), BF16),
+            pltpu.VMEM((ROWS, 16, 32, 128), BF16),
             dma((11,)),
             dma((3,)),
             dma, dma((3,)),

time: 66.4 us -> 64.8 us (0.976)
  Pallas kernels: 61.8 us -> 60.6 us
    pallas_call x1, Pallas kernels: 61.8 us -> 60.6 us  [on_device(): pl.pallas_call(main_kernel, name='gather_and_compute', out_shape=jax.Shap...]
where the time goes in v4:
time: 64.8 us; the launch traced here: 63.9 us
  Pallas kernels  60.6 us (94%)
  local copies, waits for them, and re-layouts  3.22 us (5%)
    pallas_call x1, Pallas kernels, on_device(): pl.pallas_call(main_kernel, name='gather_and_compute', out_shape=jax.Shap...  60.6 us
    unnamed x1, local copies, waits for them, and re-layouts  3.22 us

profile of v4, /device:TPU:2, one launch (start us, length us, event | category | flops | bytes accessed | tf_op | source)
XLA Modules:
  0.0 63.9 jit_solution(3426569424223422892)
XLA Ops:
  0.0 60.6 %gather_and_compute.1 = bf16[48,192,128]{2,1,0:T(8,128)(2,1)} custom-call(s32[512]{0:T(512)} %sv_hbm.1, s32[4,128]{1,0:T(4,128)} %bitcast.12, s32[1536]{0:T(1024)} %rv_hbm.1, s32[12,128]{1,0:T(8,128)} %bitcast.9, bf16[2,64,1536]{2,1,0:T(8,128)(2,1)} %bitcast.8, f32[1,64]{1,0:T(1,128)} %bitcast.13, f32[1,64]{1,0:T(1,128)} %bitcast.14, ...), custom_call_target="tpu_custom_call" | custom-call | tf_op jit(solution)/shard_map/gather_and_compute/pallas_call | solution.py:405
  60.7 3.2 %copy.11 = bf16[48,192,128]{2,1,0:T(8,128)(2,1)} copy(bf16[48,192,128]{2,1,0:T(8,128)(2,1)} %gather_and_compute.1) | data formatting | bytes 4718592
